TPU v7x, 128 devices: a whole 4x4x4 slice. The times are simulated.
128 devices in a mesh: row: 8 (over x, core), col: 16 (over z, y).
Axes of the slice: x: 4, y: 4, z: 4, core: 2. Of those that a mesh axis runs over, the one named last changes fastest.
Arguments:
- loaded: bfloat16 [1536, 8192], P('col', 'row'), may hold values from -6 to 6
- positions: int32 [1536], P('col'), may hold values from 0 to 1535, as said below
- gate_weight: bfloat16 [8192, 14336], P('row', 'col'), may hold values from -0.0625 to 0.0625
- up_weight: bfloat16 [8192, 14336], P('row', 'col'), may hold values from -0.0625 to 0.0625
- down_weight: bfloat16 [14336, 8192], P('col', 'row'), may hold values from -0.046875 to 0.046875
- segment: int32 [1536], P('col'), may hold values from 0 to 7, never falling along the last dimension, each value on 1 to 384 neighbouring positions
- log_ratio: float32 [1536], P('col'), may hold values from -6 to 6
- token_grad: bfloat16 [1536, 8192], P('col', 'row'), may hold values from -48 to 48
Outputs:
- mixed: bfloat16 [1536, 8192], P('col', 'row')
- grad_inputs: bfloat16 [1536, 8192], P('col', 'row')
- grad_gate: float32 [8192, 14336], P('row', 'col')
- grad_up: float32 [8192, 14336], P('row', 'col')
- grad_down: float32 [14336, 8192], P('col', 'row')
Inputs may be any that keep to these rules, and one draw needn't show every extreme that they name: positions is a permutation of the 1536 packed positions. Loader block c holds loader rows c * 96 to (c + 1) * 96 - 1 and owner block b holds positions b * 96 to (b + 1) * 96 - 1; at most 18 rows of one loader block land in one owner block, and every draw reaches 18.
All inputs are finite; a program needn't handle non-finite values.
Results may differ from a plain program's by a relative error of at most 0.033.
Values may be sent and summed in bfloat16 or wider, within the bound.
A program may use at most 128 MiB of HBM per device.

v0:
```python
import jax
import jax.numpy as jnp
from jax import lax
from jax.experimental import pallas as pl
from jax.experimental.pallas import tpu as pltpu
from jax.sharding import PartitionSpec as P

BETA = 0.1
F32, BF16 = jnp.float32, jnp.bfloat16
TOK, DB, FB = 1536, 1024, 896
BLOCK, HALF = 96, 48
CHUNK, SHARE = 384, 48
PLANE = 192
FAR = 384
PLANE_OFF = (2, 1, -1, 0)
MINOR_OFF = (0, 1, -1, 2)
CHUNKS = (
    ((0, 0), (0, 1), (0, 2), (0, 3)),
    ((1, 0), (1, 1), (2, 2), (2, 3)),
    ((2, 0), (2, 1), (1, 2), (1, 3)),
    ((3, 0), (3, 1), (3, 2), (3, 3)),
)
NT = (((0,), (0,)), ((), ()))
TN = (((1,), (1,)), ((), ()))


def rows(start, size):
    return pl.ds(start, size)


def kernel(spots, parts, ratios, loaded, token_grad, gw, uw, dw, mixed, ginp, ggate, gup, gdown, *scratch):
    (tiles, weights, down, xl, xs, grads, pre, pre_pair, pre_r1, pre_r2, pre_share, hid, ghp, gh_pair,
     gh_r1, gh_r2, act, part_m, c1, c2, c3, onehot, onehot_far, places, totals_u, totals_d, small_u, small_s, small_f, held_grad, send, recv, local) = scratch
    part_i = xl
    row, col = lax.axis_index("row"), lax.axis_index("col")
    x, k, z, y = row // 2, row % 2, col // 4, col % 4

    def device(dx=0, dk=0, dz=0, dy=0):
        return {
            "row": lax.rem(x + dx + 4, 4) * 2 + lax.rem(k + dk, 2),
            "col": lax.rem(z + dz + 4, 4) * 4 + lax.rem(y + dy + 4, 4),
        }

    sent, gone = [], set()

    def transfer(src, dst, target, landing=None):
        index = len(sent)
        copy = pltpu.make_async_remote_copy(
            src_ref=src, dst_ref=dst, send_sem=send.at[index], recv_sem=recv.at[index],
            device_id=target, device_id_type=pl.DeviceIdType.MESH,
        )
        copy.start()
        sent.append(copy)
        if landing is None:
            return copy
        return pltpu.make_async_remote_copy(
            src_ref=src, dst_ref=landing, send_sem=send.at[index], recv_sem=recv.at[index],
            device_id=target, device_id_type=pl.DeviceIdType.MESH,
        )

    local_copies = []

    def fetch(src, dst):
        copy = pltpu.make_async_copy(src, dst, local.at[len(local_copies)])
        copy.start()
        local_copies.append(copy)
        return copy

    def along(half, major=0, minor=0):
        return device(dz=major, dy=minor) if half == 0 else device(dz=minor, dy=major)

    def place(half, plane, minor):
        for c, held in enumerate(CHUNKS):
            if (plane, minor) in held:
                return rows(c * CHUNK + half * PLANE + held.index((plane, minor)) * HALF, HALF)

    sources = (spots, parts, ratios, token_grad)
    spots, parts, ratios, token_grad = small_u, small_s, small_f, held_grad
    first_copies = [
        fetch(loaded.at[rows(half * HALF, HALF), :], xl.at[place(half, 3, 0), :]) for half in (0, 1)
    ]
    small_copies = [fetch(a, b) for a, b in zip(sources, (spots, parts, ratios, token_grad))]
    weight_copies = [fetch(gw, weights.at[:, 0:FB]), fetch(uw, weights.at[:, FB : 2 * FB]), fetch(dw, down)]

    others = [(dz, dy) for dz in range(4) for dy in range(4) if (dz, dy) != (0, 0)]
    barrier = pltpu.get_barrier_semaphore()
    peers = [device(dz=dz, dy=dy) for dz, dy in others]
    peers += [device(dx=1), device(dx=-1), device(dk=1)]
    for peer in peers:
        pl.semaphore_signal(barrier, inc=1, device_id=peer, device_id_type=pl.DeviceIdType.MESH)
    pl.semaphore_wait(barrier, len(peers))

    class Gather:
        def __init__(self, buf):
            self.buf, self.got, self.seen, self.left = buf, {}, set(), False

        def move(self, half, src, dst, target):
            self.got[(half,) + dst] = transfer(
                self.buf.at[place(half, *src)], self.buf.at[place(half, *dst)], target
            )

        def spread(self, half, minor):
            self.move(half, (3, minor), (2, minor), along(half, major=1))
            self.move(half, (3, minor), (1, minor), along(half, major=-1))

        def begin(self):
            for half in (0, 1):
                self.move(half, (3, 0), (3, 2), along(half, minor=1))
                self.move(half, (3, 0), (3, 1), along(half, minor=-1))
                self.move(half, (3, 0), (3, 3), along(half, minor=2))
                self.spread(half, 0)

        def wait(self, half, plane, minor):
            if (half, plane, minor) not in self.seen:
                self.got[(half, plane, minor)].wait_recv()
                self.seen.add((half, plane, minor))

        def spread_on(self, half, minor):
            self.wait(half, 3, minor)
            self.spread(half, minor)

        def forward(self, half, minor):
            plane, way = (2, 1) if minor < 2 else (1, -1)
            self.wait(half, plane, minor)
            self.move(half, (plane, minor), (0, minor), along(half, major=way))

        def need(self, *chunks):
            for c in chunks:
                for half in (0, 1):
                    for plane, minor in CHUNKS[c]:
                        if (plane, minor) != (3, 0):
                            self.wait(half, plane, minor)

    gather_x, gather_g = Gather(xl), Gather(grads)
    for copy in first_copies:
        copy.wait()
    tile_copies = []

    def send_tiles():
        for copy in small_copies:
            copy.wait()
        tiles[0:8, :] = jnp.full((8, 128), -1.0, F32)
        tiles[0:1, 0:BLOCK] = spots[...].astype(F32)
        tiles[1:2, 0:BLOCK] = parts[...].astype(F32)
        tiles[2:3, 0:BLOCK] = ratios[...]
        for dz, dy in others:
            slot = ((-dz) % 4) * 4 + (-dy) % 4
            tile_copies.append(
                transfer(tiles.at[0:8, :], tiles.at[slot * 8 : slot * 8 + 8, :], device(dz=dz, dy=dy))
            )

    def slot_of(half, plane, minor):
        major, less = PLANE_OFF[plane] % 4, MINOR_OFF[minor] % 4
        return major * 4 + less if half == 0 else less * 4 + major

    def tables():
        for copy in tile_copies:
            copy.wait_recv()
        table = tiles[...]
        turned = table.T
        for half in (0, 1):
            for plane in range(4):
                for minor in range(4):
                    lane = slot_of(half, plane, minor) * 8
                    column = turned[half * HALF : half * HALF + HALF, lane : lane + 1]
                    places[place(half, plane, minor), :] = jnp.broadcast_to(column, (HALF, 128)).astype(jnp.int32)
        segment_part = jnp.concatenate([table[8 * i + 1 : 8 * i + 2, :] for i in range(16)], 0)
        ratio_part = jnp.concatenate([table[8 * i + 2 : 8 * i + 3, :] for i in range(16)], 0)

        def total(s):
            return jnp.sum(jnp.where(segment_part == float(s), ratio_part, 0.0), axis=(0, 1), keepdims=True)

        own_segment = turned[0:BLOCK, 1:2]
        token_weight = jnp.zeros((BLOCK, 1), F32)
        for p in range(4):
            margin = BETA * (total(2 * p) - total(2 * p + 1))
            pair_weight = -BETA * jax.nn.sigmoid(-margin)
            token_weight = jnp.where(own_segment == float(2 * p), pair_weight, token_weight)
            token_weight = jnp.where(own_segment == float(2 * p + 1), -pair_weight, token_weight)
        for half in (0, 1):
            part = rows(half * HALF, HALF)
            weight = token_weight[half * HALF : half * HALF + HALF, :]
            grads[place(half, 3, 0), :] = (weight * token_grad[part, :].astype(F32)).astype(BF16)

    ready = []

    def need_weights():
        if not ready:
            for copy in weight_copies:
                copy.wait()
            ready.append(True)

    def tokens_of(c):
        lane = lax.broadcasted_iota(jnp.int32, (1, CHUNK), 1)
        token = lane
        for j in range(8):
            half, (plane, minor) = j // 4, CHUNKS[c][j % 4]
            major, less = PLANE_OFF[plane], MINOR_OFF[minor]
            dz, dy = (major, less) if half == 0 else (less, major)
            block = lax.rem(z + dz + 4, 4) * 4 + lax.rem(y + dy + 4, 4)
            inside = (lane >= j * HALF) & (lane < (j + 1) * HALF)
            token = token + jnp.where(inside, block * BLOCK + half * HALF - j * HALF, 0)
        return token

    def match(c, first, count, ref):
        token = tokens_of(c)

        def build(i, carry):
            part = rows(pl.multiple_of(i * 128, 128), 128)
            here = places[rows(pl.multiple_of(first + i * 128, 128), 128), :]
            for j in range(0, CHUNK, 128):
                ref[part, j : j + 128] = jnp.where(here == token[:, j : j + 128], 1.0, 0.0).astype(BF16)
            return carry

        lax.fori_loop(0, count // 128, build, 0)

    def permute_most(c):
        gather_x.need(1, 2, 3)
        match(c, FAR, TOK - FAR, onehot)
        xs[rows(c * CHUNK, CHUNK), :] = lax.dot_general(
            onehot[...], xl[FAR:TOK, :], NT, preferred_element_type=F32
        ).astype(BF16)

    def permute_rest(c):
        gather_x.need(0)
        match(c, 0, FAR, onehot_far)
        chunk = rows(c * CHUNK, CHUNK)
        rest = lax.dot_general(onehot_far[...], xl[0:FAR, :], NT, preferred_element_type=F32)
        xs[chunk, :] = (xs[chunk, :].astype(F32) + rest).astype(BF16)

    def pre_matmul(c, i):
        need_weights()
        chunk, cols = rows(c * CHUNK, CHUNK), rows(i * FB, FB)
        pre[chunk, cols] = jnp.dot(xs[chunk, :], weights[:, cols], preferred_element_type=F32).astype(BF16)
        forward[c].pair_send(i)

    def gh_matmul(c):
        need_weights()
        gather_g.need(c)
        chunk = rows(c * CHUNK, CHUNK)
        ghp[chunk, :] = lax.dot_general(grads[chunk, :], down[...], TN, preferred_element_type=F32).astype(BF16)
        backward[c].pair_send(0)

    def mixed_matmul(c):
        chunk = rows(c * CHUNK, CHUNK)
        forward[c].out_wait()
        part_m[chunk, :] = jnp.dot(hid[chunk, :], down[...], preferred_element_type=F32).astype(BF16)

    def ginp_matmul(c):
        chunk = rows(c * CHUNK, CHUNK)
        backward[c].out_wait()
        if not gather_x.left:
            gather_x.left = True
            for copy in gather_x.got.values():
                copy.wait_send()
                gone.add(id(copy))
        part_i[chunk, :] = lax.dot_general(
            act[chunk, :], weights[...], TN, preferred_element_type=F32
        ).astype(BF16)

    xp, xm, xo = lax.rem(x + 1, 4), lax.rem(x + 3, 4), lax.rem(x + 2, 4)

    class RowChunk:
        def __init__(self, c, part, pair, r1, r2, width, out, out_width):
            self.c, self.part, self.pair, self.r1, self.r2 = c, part, pair, r1, r2
            self.width, self.out, self.out_width = width, out, out_width
            self.pairs, self.far, self.near, self.last = {}, {}, {}, {}

        def cut(self, width):
            if width == 2 * FB:
                return FB
            return 512 if self.c % 2 == 0 else 384

        def mine(self, xx):
            return rows(pl.multiple_of(self.c * CHUNK + k * PLANE + xx * SHARE, 16), SHARE)

        def pair_send(self, i):
            theirs = rows(pl.multiple_of(self.c * CHUNK + (1 - k) * PLANE, 16), PLANE)
            cols = rows(i * FB, FB)
            self.pairs[i] = transfer(self.part.at[theirs, cols], self.pair.at[self.c, :, cols], device(dk=1))

        def pair_add(self, i):
            self.pairs[i].wait_recv()
            mine, cols = rows(pl.multiple_of(self.c * CHUNK + k * PLANE, 16), PLANE), rows(i * FB, FB)
            both = self.part[mine, cols].astype(F32) + self.pair[self.c, :, cols].astype(F32)
            self.part[mine, cols] = both.astype(BF16)
            cut, far = self.cut(self.width), self.mine(xo)
            for way, lo, hi, dx in ((0, 0, cut, 1), (1, cut, self.width, -1)):
                if self.width == FB or way == i:
                    self.far[way] = transfer(
                        self.part.at[far, lo:hi], self.r1.at[self.c, :, lo:hi], device(dx=dx)
                    )

        def ring_add(self, i):
            cut = self.cut(self.width)
            xx, lo, hi, dx = ((xp, 0, cut, 1), (xm, cut, self.width, -1))[i]
            self.far[i].wait_recv()
            mine = self.mine(xx)
            both = self.part[mine, lo:hi].astype(F32) + self.r1[self.c, :, lo:hi].astype(F32)
            self.part[mine, lo:hi] = both.astype(BF16)
            self.near[i] = transfer(self.part.at[mine, :], self.r2.at[self.c, i], device(dx=dx))

        def total(self):
            self.near[0].wait_recv()
            self.near[1].wait_recv()
            return (
                self.part[self.mine(x), :].astype(F32)
                + self.r2[self.c, 0].astype(F32)
                + self.r2[self.c, 1].astype(F32)
            )

        def out_send(self):
            own = self.out.at[self.mine(x), :]
            self.side = [
                transfer(own, own, device(dx=1), self.out.at[self.mine(xm), :]),
                transfer(own, own, device(dx=-1), self.out.at[self.mine(xp), :]),
            ]
            self.done = []
            self.over(x)

        def over(self, xx):
            mine = self.out.at[self.mine(xx), :]
            other = rows(pl.multiple_of(self.c * CHUNK + (1 - k) * PLANE + xx * SHARE, 16), SHARE)
            self.done.append(transfer(mine, mine, device(dk=1), self.out.at[other, :]))

        def out_forward(self, i):
            cut = self.cut(self.out_width)
            xx, lo, hi, dx = ((xm, 0, cut, 1), (xp, cut, self.out_width, -1))[i]
            self.side[i].wait_recv()
            piece = self.out.at[self.mine(xx), lo:hi]
            self.last[i] = transfer(piece, piece, device(dx=dx), self.out.at[self.mine(xo), lo:hi])
            self.over(xx)

        def out_pair(self):
            self.last[0].wait_recv()
            self.last[1].wait_recv()
            self.over(xo)

        def out_wait(self):
            for copy in self.done:
                copy.wait_recv()
            self.done = []

    forward = [RowChunk(c, pre, pre_pair, pre_r1, pre_r2, 2 * FB, hid, FB) for c in range(4)]
    backward = [RowChunk(c, ghp, gh_pair, gh_r1, gh_r2, FB, act, 2 * FB) for c in range(4)]

    def hidden(c):
        both = forward[c].total()
        pre_share[c] = both
        gate, up = both[:, :FB], both[:, FB:]
        hid[forward[c].mine(x), :] = (gate * jax.nn.sigmoid(gate) * up).astype(BF16)
        forward[c].out_send()

    def acts(c):
        grad = backward[c].total()
        gate, up = pre_share[c, :, 0:FB], pre_share[c, :, FB : 2 * FB]
        s = jax.nn.sigmoid(gate)
        mine = backward[c].mine(x)
        act[mine, 0:FB] = (grad * up * s * (1.0 + gate * (1.0 - s))).astype(BF16)
        act[mine, FB : 2 * FB] = (grad * gate * s).astype(BF16)
        backward[c].out_send()

    class ColSum:
        def __init__(self, half, which, part, out):
            self.half, self.part, self.out = half, part, out
            self.c1, self.c2, self.c3 = c1.at[which], c2.at[which], c3.at[which]

        def part_of(self, c, i):
            return rows(c * CHUNK + self.half * PLANE + i * 96, 96)

        def near_send(self, c, i, way):
            to = 0 if way == 1 else 1
            self.near.append(
                transfer(
                    self.part.at[self.part_of(c, i), :],
                    self.c2.at[to, i * 96 : i * 96 + 96, :],
                    along(self.half, major=way),
                )
            )

        def send_far(self):
            self.far = [
                transfer(self.part.at[self.part_of(0, i), :], self.c1.at[i], along(self.half, major=1 - 2 * i))
                for i in (0, 1)
            ]
            self.near = []

        def send_near(self, i):
            self.far[i].wait_recv()
            mine = self.part_of(1, i)
            self.part[mine, :] = (self.part[mine, :].astype(F32) + self.c1[i].astype(F32)).astype(BF16)
            self.near_send(1, i, 1 - 2 * i)

        def send_rest(self):
            self.near_send(2, 0, -1)
            self.near_send(2, 1, 1)

        def send_minor(self):
            for copy in self.near:
                copy.wait_recv()
            start = 3 * CHUNK + self.half * PLANE
            own = rows(start, PLANE)
            self.part[own, :] = (
                self.part[own, :].astype(F32) + self.c2[0].astype(F32) + self.c2[1].astype(F32)
            ).astype(BF16)
            self.minor = [
                transfer(
                    self.part.at[rows(start + m * HALF, HALF), :],
                    self.c3.at[m - 1],
                    along(self.half, minor=MINOR_OFF[m]),
                )
                for m in (1, 2, 3)
            ]

        def store(self):
            total = self.part[rows(3 * CHUNK + self.half * PLANE, HALF), :].astype(F32)
            for i in range(3):
                self.minor[i].wait_recv()
                total = total + self.c3[i].astype(F32)
            self.out[rows(self.half * HALF, HALF), :] = total.astype(BF16)

    mixed_sum = [ColSum(h, h, part_m, mixed) for h in (0, 1)]
    ginp_sum = [ColSum(h, 2 + h, part_i, ginp) for h in (0, 1)]

    stores = []

    def tile(i):
        return rows(pl.multiple_of(i * 256, 256), 256)

    def keep(which, i, src, dst):
        copy = pltpu.make_async_copy(src, dst, local.at[16 + which * 4 + i])
        copy.start()
        return copy

    def down_grad(first):
        part = rows(first * CHUNK, 2 * CHUNK)
        gather_g.need(first, first + 1)
        for c in (first, first + 1):
            forward[c].out_wait()

        def body(i, carry):
            new = lax.dot_general(hid[part, :], grads[part, tile(i)], NT, preferred_element_type=F32)
            totals_d[i] = totals_d[i] + new if first else new
            if first:
                keep(2, i, totals_d.at[i], gdown.at[:, tile(i)])
            return carry

        lax.fori_loop(0, 4, body, 0)
        if first:
            for i in range(4):
                stores.append((2, i, totals_d.at[i], gdown.at[:, rows(i * 256, 256)]))

    def up_grad(which, first):
        part, wide = rows(first * CHUNK, 2 * CHUNK), rows(which * FB, FB)
        target = (ggate, gup)[which]
        for c in (first, first + 1):
            backward[c].out_wait()

        def body(i, carry):
            new = lax.dot_general(xs[part, tile(i)], act[part, wide], NT, preferred_element_type=F32)
            totals_u[tile(i), wide] = totals_u[tile(i), wide] + new if first else new
            if first:
                keep(which, i, totals_u.at[tile(i), wide], target.at[tile(i), :])
            return carry

        lax.fori_loop(0, 4, body, 0)
        if first:
            for i in range(4):
                cols = rows(i * 256, 256)
                stores.append((which, i, totals_u.at[cols, wide], target.at[cols, :]))

    gather_x.begin()
    send_tiles()
    gather_x.spread_on(0, 2)
    gather_x.forward(0, 0)
    gather_x.spread_on(0, 1)
    gather_x.spread_on(0, 3)
    gather_x.spread_on(1, 2)
    gather_x.spread_on(1, 1)
    gather_x.spread_on(1, 3)
    gather_x.forward(1, 0)
    tables()
    gather_x.forward(0, 2)
    gather_x.forward(1, 2)
    gather_x.forward(1, 1)
    gather_x.forward(1, 3)
    gather_x.forward(0, 3)
    gather_x.forward(0, 1)
    gather_g.begin()
    permute_most(2)
    permute_most(0)
    permute_rest(0)
    pre_matmul(0, 0)
    gather_g.spread_on(0, 1)
    pre_matmul(0, 1)
    permute_rest(2)
    gather_g.spread_on(0, 3)
    gather_g.spread_on(1, 1)
    pre_matmul(2, 0)
    pre_matmul(2, 1)
    gather_g.spread_on(1, 3)
    gather_g.spread_on(0, 2)
    forward[0].pair_add(0)
    forward[2].pair_add(0)
    forward[0].pair_add(1)
    gather_g.forward(0, 0)
    gather_g.forward(0, 1)
    forward[2].pair_add(1)
    gather_g.forward(1, 0)
    gather_g.forward(1, 1)
    gather_g.spread_on(1, 2)
    permute_most(1)
    permute_rest(1)
    forward[0].ring_add(0)
    forward[0].ring_add(1)
    gather_g.forward(1, 3)
    gather_g.forward(0, 3)
    pre_matmul(1, 0)
    forward[2].ring_add(0)
    gather_g.forward(0, 2)
    forward[2].ring_add(1)
    pre_matmul(1, 1)
    forward[1].pair_add(0)
    gather_g.forward(1, 2)
    gh_matmul(2)
    gh_matmul(3)
    forward[1].pair_add(1)
    hidden(0)
    backward[2].pair_add(0)
    gh_matmul(1)
    backward[3].pair_add(0)
    gh_matmul(0)
    permute_most(3)
    backward[0].pair_add(0)
    backward[1].pair_add(0)
    forward[1].ring_add(0)
    forward[1].ring_add(1)
    hidden(2)
    permute_rest(3)
    pre_matmul(3, 0)
    backward[2].ring_add(0)
    backward[2].ring_add(1)
    forward[0].out_forward(0)
    forward[0].out_forward(1)
    pre_matmul(3, 1)
    forward[3].pair_add(0)
    backward[3].ring_add(1)
    backward[3].ring_add(0)
    backward[0].ring_add(0)
    backward[0].ring_add(1)
    backward[1].ring_add(0)
    backward[1].ring_add(1)
    forward[3].pair_add(1)
    hidden(1)
    forward[2].out_forward(0)
    forward[2].out_forward(1)
    acts(2)
    forward[0].out_pair()
    mixed_matmul(0)
    forward[3].ring_add(0)
    mixed_sum[0].send_far()
    mixed_sum[1].send_far()
    acts(0)
    acts(1)
    forward[3].ring_add(1)
    forward[1].out_forward(0)
    forward[1].out_forward(1)
    forward[2].out_pair()
    mixed_matmul(2)
    mixed_sum[1].send_rest()
    mixed_sum[0].send_rest()
    backward[2].out_forward(0)
    backward[2].out_forward(1)
    backward[0].out_forward(1)
    backward[0].out_forward(0)
    backward[1].out_forward(1)
    backward[1].out_forward(0)
    hidden(3)
    acts(3)
    forward[1].out_pair()
    mixed_matmul(1)
    mixed_sum[0].send_near(0)
    backward[2].out_pair()
    mixed_sum[1].send_near(0)
    mixed_sum[1].send_near(1)
    mixed_sum[0].send_near(1)
    down_grad(0)
    backward[0].out_pair()
    ginp_matmul(2)
    backward[1].out_pair()
    ginp_matmul(0)
    ginp_sum[1].send_far()
    ginp_sum[0].send_far()
    ginp_matmul(1)
    ginp_sum[0].send_rest()
    forward[3].out_forward(0)
    forward[3].out_forward(1)
    ginp_sum[1].send_rest()
    up_grad(0, 0)
    backward[3].out_forward(1)
    ginp_sum[1].send_near(1)
    ginp_sum[0].send_near(1)
    ginp_sum[1].send_near(0)
    ginp_sum[0].send_near(0)
    forward[3].out_pair()
    backward[3].out_forward(0)
    up_grad(1, 0)
    mixed_matmul(3)
    down_grad(2)
    mixed_sum[0].send_minor()
    backward[3].out_pair()
    mixed_sum[1].send_minor()
    ginp_matmul(3)
    ginp_sum[0].send_minor()
    ginp_sum[1].send_minor()
    up_grad(0, 2)
    mixed_sum[1].store()
    mixed_sum[0].store()
    up_grad(1, 2)
    ginp_sum[1].store()
    ginp_sum[0].store()
    for which, i, src, dst in stores:
        pltpu.make_async_copy(src, dst, local.at[16 + which * 4 + i]).wait()
    for copy in sent:
        if id(copy) not in gone:
            copy.wait_send()


STEPS = 4


def hand_over(*refs):
    for src, dst in zip(refs[:5], refs[5:]):
        dst[...] = src[...]


def per_device(loaded, positions, gate_weight, up_weight, down_weight, segment, log_ratio, token_grad):
    vmem, anywhere = pl.BlockSpec(memory_space=pltpu.VMEM), pl.BlockSpec(memory_space=pl.ANY)
    shape = jax.ShapeDtypeStruct
    buf = lambda *s: pltpu.VMEM(s, BF16)
    transfers = 220
    scratch = [
        pltpu.VMEM((128, 128), F32),
        buf(DB, 2 * FB),
        buf(FB, DB),
        buf(TOK, DB),
        buf(TOK, DB),
        buf(TOK, DB),
        buf(TOK, 2 * FB),
        buf(4, PLANE, 2 * FB),
        buf(4, SHARE, 2 * FB),
        buf(4, 2, SHARE, 2 * FB),
        pltpu.VMEM((4, SHARE, 2 * FB), F32),
        buf(TOK, FB),
        buf(TOK, FB),
        buf(4, PLANE, FB),
        buf(4, SHARE, FB),
        buf(4, 2, SHARE, FB),
        buf(TOK, 2 * FB),
        buf(TOK, DB),
        buf(4, 2, 96, DB),
        buf(4, 2, PLANE, DB),
        buf(4, 3, HALF, DB),
        buf(TOK - FAR, CHUNK),
        buf(FAR, CHUNK),
        pltpu.VMEM((TOK, 128), jnp.int32),
        pltpu.VMEM((DB, 2 * FB), F32),
        pltpu.VMEM((4, FB, 256), F32),
        pltpu.VMEM((1, BLOCK), jnp.int32),
        pltpu.VMEM((1, BLOCK), jnp.int32),
        pltpu.VMEM((1, BLOCK), F32),
        buf(BLOCK, DB),
        pltpu.SemaphoreType.DMA((transfers,)),
        pltpu.SemaphoreType.DMA((transfers,)),
        pltpu.SemaphoreType.DMA((32,)),
    ]
    outs = pl.pallas_call(
        kernel,
        out_shape=(
            shape((BLOCK, DB), BF16),
            shape((BLOCK, DB), BF16),
            shape((DB, FB), F32),
            shape((DB, FB), F32),
            shape((FB, DB), F32),
        ),
        in_specs=[anywhere] * 8,
        out_specs=[vmem] * 2 + [anywhere] * 3,
        scratch_shapes=scratch,
        compiler_params=pltpu.CompilerParams(
            collective_id=0, has_side_effects=True, vmem_limit_bytes=64 * 1024 * 1024
        ),
        name="feed_forward",
    )(
        positions.reshape(1, BLOCK), segment.reshape(1, BLOCK), log_ratio.reshape(1, BLOCK),
        loaded, token_grad, gate_weight, up_weight, down_weight,
    )
    blocks = [pl.BlockSpec((BLOCK // 2, DB), lambda i: (jnp.minimum(i, 1), 0))] * 2
    blocks += [pl.BlockSpec((o.shape[0] // STEPS, o.shape[1]), lambda i: (i, 0)) for o in outs[2:]]
    return pl.pallas_call(
        hand_over,
        grid=(STEPS,),
        out_shape=tuple(shape(o.shape, o.dtype) for o in outs),
        in_specs=blocks,
        out_specs=blocks,
        compiler_params=pltpu.CompilerParams(vmem_limit_bytes=64 * 1024 * 1024),
        name="hand_over",
    )(*outs)


def solution(mesh):
    return jax.shard_map(
        per_device,
        mesh=mesh,
        in_specs=(
            P("col", "row"),
            P("col"),
            P("row", "col"),
            P("row", "col"),
            P("col", "row"),
            P("col"),
            P("col"),
            P("col", "row"),
        ),
        out_specs=(
            P("col", "row"),
            P("col", "row"),
            P("row", "col"),
            P("row", "col"),
            P("col", "row"),
        ),
        check_vma=False,
    )
```

profile of v0, /device:TPU:0, one launch (start us, length us, event | category | flops | bytes accessed | tf_op | source)
XLA Modules:
  0.0 140.9 jit_solution(4670584375309382225)
XLA Ops:
  0.6 131.6 %feed_forward.1 = (bf16[96,1024]{1,0:T(8,128)(2,1)}, bf16[96,1024]{1,0:T(8,128)(2,1)}, f32[1024,896]{1,0:T(8,128)}, f32[1024,896]{1,0:T(8,128)}, f32[896,1024]{1,0:T(8,128)}) custom-call(s32[1,96]{1,0:T(1,128)} %bitcast.3, s32[1,96]{1,0:T(1,128)} %bitcast.4, f32[1,96]{1,0:T(1,128)} %bitcast.5, bf16[96,1024]{1,0:T(8,128)(2,1)} %loaded.1, ...), custom_call_target="tpu_custom_call" | custom-call | tf_op jit(solution)/shard_map/feed_forward/pallas_call | solution.py:677
  132.2 8.7 %hand_over.1 = (bf16[96,1024]{1,0:T(8,128)(2,1)}, bf16[96,1024]{1,0:T(8,128)(2,1)}, f32[1024,896]{1,0:T(8,128)}, f32[1024,896]{1,0:T(8,128)}, f32[896,1024]{1,0:T(8,128)}) custom-call(bf16[96,1024]{1,0:T(8,128)(2,1)} %get-tuple-element.10.refs_0_, bf16[96,1024]{1,0:T(8,128)(2,1)} %get-tuple-element.11.refs_1_, f32[1024,896]{1,0:T(8,128)} %get-tuple-element.12.refs_2_, ...), custom_call_target="tpu_custom_call" | custom-call | tf_op jit(solution)/shard_map/hand_over/pallas_call | solution.py:699
where the time goes:
time: 142 us; the launch traced here: 141 us
  Pallas kernels  140 us (99%)
    pallas_call x1, Pallas kernels, per_device(): pl.pallas_call(kernel, out_shape=(shape((BLOCK, DB), BF16), shape((BLOCK,...  132 us
    pallas_call x1, Pallas kernels, per_device(): pl.pallas_call(hand_over, grid=(STEPS,), out_shape=tuple((shape(o.shape,...  8.67 us

commit v1 on v0

--- a/solution.py
+++ b/solution.py
@@ -362,7 +362,7 @@
 
     class ColSum:
         def __init__(self, half, which, part, out):
-            self.half, self.part, self.out = half, part, out
+            self.half, self.part, self.out, self.near = half, part, out, []
             self.c1, self.c2, self.c3 = c1.at[which], c2.at[which], c3.at[which]
 
         def part_of(self, c, i):
@@ -383,7 +383,6 @@
                 transfer(self.part.at[self.part_of(0, i), :], self.c1.at[i], along(self.half, major=1 - 2 * i))
                 for i in (0, 1)
             ]
-            self.near = []
 
         def send_near(self, i):
             self.far[i].wait_recv()
@@ -472,151 +471,151 @@
     gather_x.begin()
     send_tiles()
     gather_x.spread_on(0, 2)
+    gather_x.spread_on(0, 1)
     gather_x.forward(0, 0)
-    gather_x.spread_on(0, 1)
+    gather_x.spread_on(1, 1)
     gather_x.spread_on(0, 3)
     gather_x.spread_on(1, 2)
-    gather_x.spread_on(1, 1)
+    gather_x.forward(1, 0)
     gather_x.spread_on(1, 3)
-    gather_x.forward(1, 0)
     tables()
+    gather_x.forward(1, 1)
     gather_x.forward(0, 2)
+    gather_x.forward(0, 1)
     gather_x.forward(1, 2)
-    gather_x.forward(1, 1)
+    gather_x.forward(0, 3)
     gather_x.forward(1, 3)
-    gather_x.forward(0, 3)
-    gather_x.forward(0, 1)
     gather_g.begin()
-    permute_most(2)
+    permute_most(1)
     permute_most(0)
     permute_rest(0)
+    pre_matmul(0, 1)
+    gather_g.spread_on(0, 1)
+    gather_g.forward(0, 0)
     pre_matmul(0, 0)
-    gather_g.spread_on(0, 1)
-    pre_matmul(0, 1)
+    gather_g.spread_on(1, 1)
+    forward[0].pair_add(1)
+    gather_g.spread_on(0, 3)
+    gather_g.spread_on(0, 2)
+    gather_g.spread_on(1, 2)
+    permute_rest(1)
+    forward[0].pair_add(0)
+    gather_g.spread_on(1, 3)
+    pre_matmul(1, 0)
+    gh_matmul(3)
+    forward[0].ring_add(1)
+    gather_g.forward(1, 1)
+    gather_g.forward(0, 1)
+    forward[1].pair_add(0)
+    gather_g.forward(1, 0)
+    pre_matmul(1, 1)
+    forward[0].ring_add(0)
+    gather_g.forward(0, 3)
+    gather_g.forward(1, 2)
+    backward[3].pair_add(0)
+    permute_most(2)
+    gather_g.forward(1, 3)
+    forward[1].pair_add(1)
+    forward[1].ring_add(0)
+    gh_matmul(2)
     permute_rest(2)
-    gather_g.spread_on(0, 3)
-    gather_g.spread_on(1, 1)
+    backward[3].ring_add(1)
+    gh_matmul(1)
+    gather_g.forward(0, 2)
+    hidden(0)
+    forward[1].ring_add(1)
+    backward[2].pair_add(0)
+    backward[3].ring_add(0)
+    permute_most(3)
+    backward[1].pair_add(0)
+    permute_rest(3)
+    forward[0].out_forward(1)
+    gh_matmul(0)
+    backward[2].ring_add(0)
+    forward[0].out_forward(0)
+    hidden(1)
+    backward[2].ring_add(1)
+    backward[0].pair_add(0)
+    backward[1].ring_add(1)
+    backward[1].ring_add(0)
+    forward[1].out_forward(1)
+    forward[0].out_pair()
+    mixed_matmul(0)
+    forward[1].out_forward(0)
+    mixed_sum[1].send_far()
+    backward[0].ring_add(1)
+    backward[0].ring_add(0)
+    pre_matmul(2, 1)
     pre_matmul(2, 0)
-    pre_matmul(2, 1)
-    gather_g.spread_on(1, 3)
-    gather_g.spread_on(0, 2)
-    forward[0].pair_add(0)
+    acts(1)
+    mixed_sum[0].send_far()
+    forward[2].pair_add(1)
+    forward[1].out_pair()
     forward[2].pair_add(0)
-    forward[0].pair_add(1)
-    gather_g.forward(0, 0)
-    gather_g.forward(0, 1)
-    forward[2].pair_add(1)
-    gather_g.forward(1, 0)
-    gather_g.forward(1, 1)
-    gather_g.spread_on(1, 2)
-    permute_most(1)
-    permute_rest(1)
-    forward[0].ring_add(0)
-    forward[0].ring_add(1)
-    gather_g.forward(1, 3)
-    gather_g.forward(0, 3)
-    pre_matmul(1, 0)
+    down_grad(0)
+    acts(0)
+    mixed_matmul(1)
+    mixed_sum[1].send_near(0)
+    mixed_sum[1].send_near(1)
+    backward[1].out_forward(1)
+    backward[1].out_forward(0)
+    mixed_sum[0].send_near(1)
+    mixed_sum[0].send_near(0)
+    forward[2].ring_add(1)
     forward[2].ring_add(0)
-    gather_g.forward(0, 2)
-    forward[2].ring_add(1)
-    pre_matmul(1, 1)
-    forward[1].pair_add(0)
-    gather_g.forward(1, 2)
-    gh_matmul(2)
-    gh_matmul(3)
-    forward[1].pair_add(1)
-    hidden(0)
-    backward[2].pair_add(0)
-    gh_matmul(1)
-    backward[3].pair_add(0)
-    gh_matmul(0)
-    permute_most(3)
-    backward[0].pair_add(0)
-    backward[1].pair_add(0)
-    forward[1].ring_add(0)
-    forward[1].ring_add(1)
+    backward[0].out_forward(1)
+    backward[0].out_forward(0)
+    pre_matmul(3, 1)
+    pre_matmul(3, 0)
+    backward[1].out_pair()
+    forward[3].pair_add(1)
+    forward[3].pair_add(0)
+    ginp_matmul(1)
     hidden(2)
-    permute_rest(3)
-    pre_matmul(3, 0)
-    backward[2].ring_add(0)
-    backward[2].ring_add(1)
-    forward[0].out_forward(0)
-    forward[0].out_forward(1)
-    pre_matmul(3, 1)
-    forward[3].pair_add(0)
-    backward[3].ring_add(1)
-    backward[3].ring_add(0)
-    backward[0].ring_add(0)
-    backward[0].ring_add(1)
-    backward[1].ring_add(0)
-    backward[1].ring_add(1)
-    forward[3].pair_add(1)
-    hidden(1)
+    acts(2)
+    backward[0].out_pair()
+    ginp_matmul(0)
+    forward[3].ring_add(1)
+    ginp_sum[1].send_far()
+    forward[3].ring_add(0)
+    ginp_sum[0].send_far()
+    up_grad(0, 0)
+    up_grad(1, 0)
     forward[2].out_forward(0)
     forward[2].out_forward(1)
-    acts(2)
-    forward[0].out_pair()
-    mixed_matmul(0)
-    forward[3].ring_add(0)
-    mixed_sum[0].send_far()
-    mixed_sum[1].send_far()
-    acts(0)
-    acts(1)
-    forward[3].ring_add(1)
-    forward[1].out_forward(0)
-    forward[1].out_forward(1)
+    backward[2].out_forward(1)
+    backward[2].out_forward(0)
+    ginp_sum[1].send_near(0)
+    ginp_sum[1].send_near(1)
+    ginp_sum[0].send_near(0)
+    ginp_sum[0].send_near(1)
+    hidden(3)
+    acts(3)
     forward[2].out_pair()
     mixed_matmul(2)
+    backward[2].out_pair()
+    mixed_sum[0].send_rest()
     mixed_sum[1].send_rest()
-    mixed_sum[0].send_rest()
-    backward[2].out_forward(0)
-    backward[2].out_forward(1)
-    backward[0].out_forward(1)
-    backward[0].out_forward(0)
-    backward[1].out_forward(1)
-    backward[1].out_forward(0)
-    hidden(3)
-    acts(3)
-    forward[1].out_pair()
-    mixed_matmul(1)
-    mixed_sum[0].send_near(0)
-    backward[2].out_pair()
-    mixed_sum[1].send_near(0)
-    mixed_sum[1].send_near(1)
-    mixed_sum[0].send_near(1)
-    down_grad(0)
-    backward[0].out_pair()
+    forward[3].out_forward(1)
+    forward[3].out_forward(0)
     ginp_matmul(2)
-    backward[1].out_pair()
-    ginp_matmul(0)
-    ginp_sum[1].send_far()
-    ginp_sum[0].send_far()
-    ginp_matmul(1)
     ginp_sum[0].send_rest()
-    forward[3].out_forward(0)
-    forward[3].out_forward(1)
     ginp_sum[1].send_rest()
-    up_grad(0, 0)
     backward[3].out_forward(1)
-    ginp_sum[1].send_near(1)
-    ginp_sum[0].send_near(1)
-    ginp_sum[1].send_near(0)
-    ginp_sum[0].send_near(0)
+    backward[3].out_forward(0)
     forward[3].out_pair()
-    backward[3].out_forward(0)
-    up_grad(1, 0)
     mixed_matmul(3)
-    down_grad(2)
+    mixed_sum[1].send_minor()
     mixed_sum[0].send_minor()
     backward[3].out_pair()
-    mixed_sum[1].send_minor()
+    down_grad(2)
     ginp_matmul(3)
+    ginp_sum[1].send_minor()
     ginp_sum[0].send_minor()
-    ginp_sum[1].send_minor()
+    up_grad(1, 2)
+    mixed_sum[1].store()
     up_grad(0, 2)
-    mixed_sum[1].store()
     mixed_sum[0].store()
-    up_grad(1, 2)
     ginp_sum[1].store()
     ginp_sum[0].store()
     for which, i, src, dst in stores:

time: 142 us -> 134 us (0.944)
  Pallas kernels: 140 us -> 133 us
    pallas_call x1, Pallas kernels: 132 us -> 124 us  [per_device(): pl.pallas_call(kernel, out_shape=(shape((BLOCK, DB), BF16), shape((BLOCK,...]
where the time goes in v1:
time: 134 us
  Pallas kernels  133 us (99%)
    pallas_call x1, Pallas kernels, per_device(): pl.pallas_call(kernel, out_shape=(shape((BLOCK, DB), BF16), shape((BLOCK,...  124 us
    pallas_call x1, Pallas kernels, per_device(): pl.pallas_call(hand_over, grid=(STEPS,), out_shape=tuple((shape(o.shape,...  8.67 us

profile of v1, /device:TPU:0, one launch (start us, length us, event | category | flops | bytes accessed | tf_op | source)
XLA Modules:
  0.0 133.6 jit_solution(6297603385407999644)
XLA Ops:
  0.6 124.2 %feed_forward.1 = (bf16[96,1024]{1,0:T(8,128)(2,1)}, bf16[96,1024]{1,0:T(8,128)(2,1)}, f32[1024,896]{1,0:T(8,128)}, f32[1024,896]{1,0:T(8,128)}, f32[896,1024]{1,0:T(8,128)}) custom-call(s32[1,96]{1,0:T(1,128)} %bitcast.3, s32[1,96]{1,0:T(1,128)} %bitcast.4, f32[1,96]{1,0:T(1,128)} %bitcast.5, bf16[96,1024]{1,0:T(8,128)(2,1)} %loaded.1, ...), custom_call_target="tpu_custom_call" | custom-call | tf_op jit(solution)/shard_map/feed_forward/pallas_call | solution.py:676
  124.9 8.7 %hand_over.1 = (bf16[96,1024]{1,0:T(8,128)(2,1)}, bf16[96,1024]{1,0:T(8,128)(2,1)}, f32[1024,896]{1,0:T(8,128)}, f32[1024,896]{1,0:T(8,128)}, f32[896,1024]{1,0:T(8,128)}) custom-call(bf16[96,1024]{1,0:T(8,128)(2,1)} %get-tuple-element.10.refs_0_, bf16[96,1024]{1,0:T(8,128)(2,1)} %get-tuple-element.11.refs_1_, f32[1024,896]{1,0:T(8,128)} %get-tuple-element.12.refs_2_, ...), custom_call_target="tpu_custom_call" | custom-call | tf_op jit(solution)/shard_map/hand_over/pallas_call | solution.py:698

commit v2 on v0

--- a/solution.py
+++ b/solution.py
@@ -362,7 +362,7 @@
 
     class ColSum:
         def __init__(self, half, which, part, out):
-            self.half, self.part, self.out = half, part, out
+            self.half, self.part, self.out, self.near = half, part, out, []
             self.c1, self.c2, self.c3 = c1.at[which], c2.at[which], c3.at[which]
 
         def part_of(self, c, i):
@@ -383,7 +383,6 @@
                 transfer(self.part.at[self.part_of(0, i), :], self.c1.at[i], along(self.half, major=1 - 2 * i))
                 for i in (0, 1)
             ]
-            self.near = []
 
         def send_near(self, i):
             self.far[i].wait_recv()
@@ -470,155 +469,155 @@
                 stores.append((which, i, totals_u.at[cols, wide], target.at[cols, :]))
 
     gather_x.begin()
+    gather_x.spread_on(1, 2)
+    gather_x.spread_on(0, 1)
     send_tiles()
+    gather_x.spread_on(0, 3)
+    gather_x.spread_on(1, 3)
+    gather_x.spread_on(1, 1)
     gather_x.spread_on(0, 2)
+    tables()
     gather_x.forward(0, 0)
-    gather_x.spread_on(0, 1)
-    gather_x.spread_on(0, 3)
-    gather_x.spread_on(1, 2)
-    gather_x.spread_on(1, 1)
-    gather_x.spread_on(1, 3)
     gather_x.forward(1, 0)
-    tables()
-    gather_x.forward(0, 2)
+    gather_x.forward(0, 1)
     gather_x.forward(1, 2)
-    gather_x.forward(1, 1)
     gather_x.forward(1, 3)
     gather_x.forward(0, 3)
-    gather_x.forward(0, 1)
+    gather_x.forward(1, 1)
+    gather_x.forward(0, 2)
     gather_g.begin()
+    permute_most(0)
     permute_most(2)
-    permute_most(0)
     permute_rest(0)
+    pre_matmul(0, 1)
     pre_matmul(0, 0)
-    gather_g.spread_on(0, 1)
-    pre_matmul(0, 1)
     permute_rest(2)
-    gather_g.spread_on(0, 3)
-    gather_g.spread_on(1, 1)
+    forward[0].pair_add(1)
     pre_matmul(2, 0)
+    forward[0].pair_add(0)
     pre_matmul(2, 1)
     gather_g.spread_on(1, 3)
+    forward[2].pair_add(0)
     gather_g.spread_on(0, 2)
-    forward[0].pair_add(0)
-    forward[2].pair_add(0)
-    forward[0].pair_add(1)
-    gather_g.forward(0, 0)
-    gather_g.forward(0, 1)
     forward[2].pair_add(1)
-    gather_g.forward(1, 0)
-    gather_g.forward(1, 1)
     gather_g.spread_on(1, 2)
-    permute_most(1)
-    permute_rest(1)
+    gather_g.spread_on(0, 3)
     forward[0].ring_add(0)
     forward[0].ring_add(1)
+    gh_matmul(3)
+    permute_most(1)
+    gather_g.spread_on(0, 1)
     gather_g.forward(1, 3)
+    forward[2].ring_add(0)
+    permute_rest(1)
+    forward[2].ring_add(1)
     gather_g.forward(0, 3)
+    gather_g.spread_on(1, 1)
     pre_matmul(1, 0)
-    forward[2].ring_add(0)
+    pre_matmul(1, 1)
+    hidden(0)
+    gather_g.forward(0, 1)
     gather_g.forward(0, 2)
-    forward[2].ring_add(1)
-    pre_matmul(1, 1)
+    gather_g.forward(1, 2)
+    forward[1].pair_add(1)
+    gather_g.forward(1, 1)
     forward[1].pair_add(0)
-    gather_g.forward(1, 2)
-    gh_matmul(2)
-    gh_matmul(3)
-    forward[1].pair_add(1)
-    hidden(0)
-    backward[2].pair_add(0)
+    gather_g.forward(0, 0)
+    gather_g.forward(1, 0)
+    hidden(2)
+    forward[0].out_forward(0)
     gh_matmul(1)
-    backward[3].pair_add(0)
+    forward[0].out_forward(1)
+    backward[1].pair_add(0)
+    forward[1].ring_add(1)
+    forward[1].ring_add(0)
     gh_matmul(0)
     permute_most(3)
     backward[0].pair_add(0)
-    backward[1].pair_add(0)
-    forward[1].ring_add(0)
-    forward[1].ring_add(1)
-    hidden(2)
+    forward[2].out_forward(0)
+    backward[1].ring_add(0)
+    forward[0].out_pair()
+    backward[1].ring_add(1)
+    forward[2].out_forward(1)
+    mixed_matmul(0)
+    backward[0].ring_add(1)
+    hidden(1)
+    backward[0].ring_add(0)
+    forward[2].out_pair()
+    acts(1)
+    mixed_matmul(2)
+    forward[1].out_forward(0)
     permute_rest(3)
     pre_matmul(3, 0)
+    acts(0)
+    pre_matmul(3, 1)
+    mixed_sum[1].send_far()
+    gh_matmul(2)
+    backward[1].out_forward(0)
+    forward[1].out_forward(1)
+    backward[2].pair_add(0)
+    forward[3].pair_add(1)
+    backward[0].out_forward(1)
+    backward[1].out_forward(1)
+    mixed_sum[0].send_far()
+    backward[0].out_forward(0)
+    backward[3].pair_add(0)
+    forward[1].out_pair()
+    mixed_matmul(1)
+    backward[2].ring_add(1)
+    forward[3].pair_add(0)
     backward[2].ring_add(0)
-    backward[2].ring_add(1)
-    forward[0].out_forward(0)
-    forward[0].out_forward(1)
-    pre_matmul(3, 1)
-    forward[3].pair_add(0)
+    mixed_sum[0].send_rest()
+    mixed_sum[1].send_near(0)
+    forward[3].ring_add(1)
+    mixed_sum[0].send_near(1)
+    backward[0].out_pair()
+    backward[1].out_pair()
+    mixed_sum[1].send_near(1)
+    forward[3].ring_add(0)
+    ginp_matmul(0)
+    ginp_sum[0].send_far()
+    acts(2)
+    ginp_sum[1].send_far()
+    ginp_matmul(1)
+    down_grad(0)
+    mixed_sum[0].send_near(0)
+    hidden(3)
+    up_grad(0, 0)
     backward[3].ring_add(1)
     backward[3].ring_add(0)
-    backward[0].ring_add(0)
-    backward[0].ring_add(1)
-    backward[1].ring_add(0)
-    backward[1].ring_add(1)
-    forward[3].pair_add(1)
-    hidden(1)
-    forward[2].out_forward(0)
-    forward[2].out_forward(1)
-    acts(2)
-    forward[0].out_pair()
-    mixed_matmul(0)
-    forward[3].ring_add(0)
-    mixed_sum[0].send_far()
-    mixed_sum[1].send_far()
-    acts(0)
-    acts(1)
-    forward[3].ring_add(1)
-    forward[1].out_forward(0)
-    forward[1].out_forward(1)
-    forward[2].out_pair()
-    mixed_matmul(2)
     mixed_sum[1].send_rest()
-    mixed_sum[0].send_rest()
+    ginp_sum[1].send_near(1)
+    ginp_sum[0].send_near(0)
     backward[2].out_forward(0)
     backward[2].out_forward(1)
-    backward[0].out_forward(1)
-    backward[0].out_forward(0)
-    backward[1].out_forward(1)
-    backward[1].out_forward(0)
-    hidden(3)
-    acts(3)
-    forward[1].out_pair()
-    mixed_matmul(1)
-    mixed_sum[0].send_near(0)
-    backward[2].out_pair()
-    mixed_sum[1].send_near(0)
-    mixed_sum[1].send_near(1)
-    mixed_sum[0].send_near(1)
-    down_grad(0)
-    backward[0].out_pair()
-    ginp_matmul(2)
-    backward[1].out_pair()
-    ginp_matmul(0)
-    ginp_sum[1].send_far()
-    ginp_sum[0].send_far()
-    ginp_matmul(1)
-    ginp_sum[0].send_rest()
+    up_grad(1, 0)
     forward[3].out_forward(0)
     forward[3].out_forward(1)
-    ginp_sum[1].send_rest()
-    up_grad(0, 0)
-    backward[3].out_forward(1)
-    ginp_sum[1].send_near(1)
+    acts(3)
     ginp_sum[0].send_near(1)
     ginp_sum[1].send_near(0)
-    ginp_sum[0].send_near(0)
+    backward[2].out_pair()
     forward[3].out_pair()
+    ginp_matmul(2)
+    ginp_sum[1].send_rest()
+    ginp_sum[0].send_rest()
+    mixed_matmul(3)
     backward[3].out_forward(0)
-    up_grad(1, 0)
-    mixed_matmul(3)
+    backward[3].out_forward(1)
     down_grad(2)
     mixed_sum[0].send_minor()
+    mixed_sum[1].send_minor()
     backward[3].out_pair()
-    mixed_sum[1].send_minor()
     ginp_matmul(3)
     ginp_sum[0].send_minor()
     ginp_sum[1].send_minor()
     up_grad(0, 2)
+    up_grad(1, 2)
     mixed_sum[1].store()
     mixed_sum[0].store()
-    up_grad(1, 2)
+    ginp_sum[0].store()
     ginp_sum[1].store()
-    ginp_sum[0].store()
     for which, i, src, dst in stores:
         pltpu.make_async_copy(src, dst, local.at[16 + which * 4 + i]).wait()
     for copy in sent:

time: 142 us -> 132 us (0.930)
  Pallas kernels: 140 us -> 131 us
    pallas_call x1, Pallas kernels: 132 us -> 122 us  [per_device(): pl.pallas_call(kernel, out_shape=(shape((BLOCK, DB), BF16), shape((BLOCK,...]
where the time goes in v2:
time: 132 us
  Pallas kernels  131 us (99%)
    pallas_call x1, Pallas kernels, per_device(): pl.pallas_call(kernel, out_shape=(shape((BLOCK, DB), BF16), shape((BLOCK,...  122 us
    pallas_call x1, Pallas kernels, per_device(): pl.pallas_call(hand_over, grid=(STEPS,), out_shape=tuple((shape(o.shape,...  8.67 us

profile of v2, /device:TPU:0, one launch (start us, length us, event | category | flops | bytes accessed | tf_op | source)
XLA Modules:
  0.0 131.6 jit_solution(2287084201847534579)
XLA Ops:
  0.6 122.2 %feed_forward.1 = (bf16[96,1024]{1,0:T(8,128)(2,1)}, bf16[96,1024]{1,0:T(8,128)(2,1)}, f32[1024,896]{1,0:T(8,128)}, f32[1024,896]{1,0:T(8,128)}, f32[896,1024]{1,0:T(8,128)}) custom-call(s32[1,96]{1,0:T(1,128)} %bitcast.3, s32[1,96]{1,0:T(1,128)} %bitcast.4, f32[1,96]{1,0:T(1,128)} %bitcast.5, bf16[96,1024]{1,0:T(8,128)(2,1)} %loaded.1, ...), custom_call_target="tpu_custom_call" | custom-call | tf_op jit(solution)/shard_map/feed_forward/pallas_call | solution.py:676
  122.9 8.7 %hand_over.1 = (bf16[96,1024]{1,0:T(8,128)(2,1)}, bf16[96,1024]{1,0:T(8,128)(2,1)}, f32[1024,896]{1,0:T(8,128)}, f32[1024,896]{1,0:T(8,128)}, f32[896,1024]{1,0:T(8,128)}) custom-call(bf16[96,1024]{1,0:T(8,128)(2,1)} %get-tuple-element.10.refs_0_, bf16[96,1024]{1,0:T(8,128)(2,1)} %get-tuple-element.11.refs_1_, f32[1024,896]{1,0:T(8,128)} %get-tuple-element.12.refs_2_, ...), custom_call_target="tpu_custom_call" | custom-call | tf_op jit(solution)/shard_map/hand_over/pallas_call | solution.py:698
